TPU v7x, 32 devices: a whole 2x2x4 slice. The times are simulated.
32 devices in a mesh: groups: 2 (over x), gx: 4 (over y, core), gy: 4 (over z).
Axes of the slice: x: 2, y: 2, z: 4, core: 2. Of those that a mesh axis runs over, the one named last changes fastest.
Arguments:
- hidden_state: bfloat16 [512, 8192], P('groups', 'gx'), parts along dimension 0
- cache_row: int32 [512], P('groups'), parts along dimension 0, may hold values from 0 to 255, each once
- ctx_len: int32 [512], P('groups'), parts along dimension 0, may hold values from 2 to 192, as said below
- w_query: bfloat16 [8192, 8192], P('gx', 'gy'), may hold values from -0.0625 to 0.0625
- w_key: bfloat16 [8192, 1024], P('gx', 'gy'), may hold values from -0.0625 to 0.0625
- w_value: bfloat16 [8192, 1024], P('gx', 'gy'), may hold values from -0.0625 to 0.0625
- w_output: bfloat16 [8192, 8192], P('gy', 'gx'), may hold values from -0.5 to 0.5
- k_cache: bfloat16 [512, 192, 1024], P(('groups', 'gx', 'gy')), parts along dimension 0
- v_cache: bfloat16 [512, 192, 1024], P(('groups', 'gx', 'gy')), parts along dimension 0, may hold values from -6 to 6
Outputs:
- mixed: bfloat16 [512, 8192], P(('groups', 'gy'), 'gx'), parts along dimension 0
There are 2 independent parts, one for each index of `groups`. A program takes and returns all parts, laid end to end along the dimension named above; an argument that names none is the same for every part. Nothing has to cross between parts.
Inputs may be any that keep to these rules, and one draw needn't show every extreme that they name: cache_row is a permutation: request r's cache lies in cache row cache_row[r], and every row holds one request. Slots 0 to ctx_len[r] - 1 of a request's cache row are valid; the new token sits at position ctx_len[r]. Some request has exactly 192.
All inputs are finite; a program needn't handle non-finite values.
Results may differ from a plain program's by a relative error of at most 0.012.
The roundings to bfloat16 on the way count: a program that leaves them out, or rounds other values in their place, can miss the bound.
Values may be sent and summed in bfloat16 or wider, within the bound.
A program may use at most 128 MiB of HBM per device.

v0:
```python
import math

import jax
import jax.numpy as jnp
from jax import lax
from jax.sharding import PartitionSpec as P

D = 8192
H = 64
KVH = 8
HD = 128


EPS = 1e-05
THETA = 500000.0


def rotate(values, position):
    half = values.shape[-1] // 2
    index = jnp.arange(half, dtype=jnp.float32)
    freq = jnp.exp(index * (-2.0 * math.log(THETA) / values.shape[-1]))
    angle = position[:, None, None] * freq[None, None, :]
    cosine = jnp.cos(angle)
    sine = jnp.sin(angle)
    first = values[..., :half]
    second = values[..., half:]
    return jnp.concatenate(
        [first * cosine - second * sine, second * cosine + first * sine], axis=-1
    )


def attend(query, key_new, value_new, key_cache, value_cache, lengths):
    count = query.shape[0]
    context = key_cache.shape[1]
    group = H // KVH
    scale = 1.0 / math.sqrt(HD)
    position = lengths.astype(jnp.float32)
    query_rot = rotate(query.astype(jnp.float32).reshape(count, H, HD), position).astype(
        jnp.bfloat16
    )
    query_rot = query_rot.reshape(count, KVH, group, HD)
    key_rot = rotate(key_new.astype(jnp.float32).reshape(count, KVH, HD), position).astype(
        jnp.bfloat16
    )
    keys = key_cache.reshape(count, context, KVH, HD)
    values = value_cache.reshape(count, context, KVH, HD)
    scores = (
        jnp.einsum("rkgd,rckd->rkgc", query_rot, keys, preferred_element_type=jnp.float32) * scale
    )
    self_score = (
        jnp.einsum("rkgd,rkd->rkg", query_rot, key_rot, preferred_element_type=jnp.float32) * scale
    )
    valid = (jnp.arange(context, dtype=jnp.int32)[None, :] < lengths[:, None])[:, None, None, :]
    highest = jnp.maximum(jnp.max(jnp.where(valid, scores, -jnp.inf), axis=-1), self_score)
    weights = jnp.where(valid, jnp.exp(scores - highest[..., None]), 0.0)
    self_weight = jnp.exp(self_score - highest)
    denominator = jnp.sum(weights, axis=-1) + self_weight
    self_prob = lax.optimization_barrier(self_weight.astype(jnp.bfloat16)).astype(jnp.float32)
    value_self = value_new.reshape(count, KVH, HD).astype(jnp.float32)
    summed = jnp.einsum(
        "rkgc,rckd->rkgd", weights.astype(jnp.bfloat16), values, preferred_element_type=jnp.float32
    )
    summed = summed + self_prob[..., None] * value_self[:, :, None, :]
    return (summed / denominator[..., None]).astype(jnp.bfloat16).reshape(count, H * HD)


def body(hidden_state, cache_row, ctx_len, w_query, w_key, w_value, w_output, k_cache, v_cache):
    request_total = cache_row.shape[0]
    inverse = (
        jnp.zeros_like(cache_row).at[cache_row].set(jnp.arange(request_total, dtype=jnp.int32))
    )
    ordered = jnp.take(hidden_state, inverse, axis=0)
    lengths = jnp.take(ctx_len, inverse)
    squares = jnp.sum(jnp.square(ordered.astype(jnp.float32)), axis=1)
    query_part = jnp.dot(ordered, w_query, preferred_element_type=jnp.float32)
    key_part = jnp.dot(ordered, w_key, preferred_element_type=jnp.float32)
    value_part = jnp.dot(ordered, w_value, preferred_element_type=jnp.float32)
    square_sums = lax.psum(squares, "gx")
    query_sum, key_sum, value_sum = (
        lax.psum_scatter(query_part, "gx", scatter_dimension=0, tiled=True),
        lax.psum_scatter(key_part, "gx", scatter_dimension=0, tiled=True),
        lax.psum_scatter(value_part, "gx", scatter_dimension=0, tiled=True),
    )
    block_rows = query_sum.shape[0]
    block_squares = lax.dynamic_slice_in_dim(
        square_sums, lax.axis_index("gx") * block_rows, block_rows
    )
    inv_rms = lax.rsqrt(block_squares / D + EPS)[:, None]
    query = (query_sum * inv_rms).astype(jnp.bfloat16)
    key_new = (key_sum * inv_rms).astype(jnp.bfloat16)
    value_new = (value_sum * inv_rms).astype(jnp.bfloat16)
    query_own, key_own, value_own = (
        lax.all_to_all(query, "gy", split_axis=0, concat_axis=1, tiled=True),
        lax.all_to_all(key_new, "gy", split_axis=0, concat_axis=1, tiled=True),
        lax.all_to_all(value_new, "gy", split_axis=0, concat_axis=1, tiled=True),
    )
    owned = k_cache.shape[0]
    first_row = (lax.axis_index("gx") * lax.axis_size("gy") + lax.axis_index("gy")) * owned
    own_lengths = lax.dynamic_slice_in_dim(lengths, first_row, owned)
    attn = attend(query_own, key_own, value_own, k_cache, v_cache, own_lengths)
    returned = lax.all_to_all(attn, "gy", split_axis=1, concat_axis=0, tiled=True)
    partial_out = jnp.dot(
        lax.all_gather(returned, "gx", axis=0, tiled=True),
        w_output,
        preferred_element_type=jnp.float32,
    )
    by_request = jnp.take(partial_out, cache_row, axis=0)
    mixed = lax.psum_scatter(by_request, "gy", scatter_dimension=0, tiled=True)
    return mixed.astype(jnp.bfloat16)


def solution(mesh):
    placed = (
        P("groups", "gx"),
        P("groups"),
        P("groups"),
        P("gx", "gy"),
        P("gx", "gy"),
        P("gx", "gy"),
        P("gy", "gx"),
        P(("groups", "gx", "gy"), None, None),
        P(("groups", "gx", "gy"), None, None),
    )
    return jax.shard_map(
        body, mesh=mesh, in_specs=placed, out_specs=P(("groups", "gy"), "gx"), check_vma=False
    )
```

profile of v0, /device:TPU:0, one launch (start us, length us, event | category | flops | bytes accessed | tf_op | source)
XLA Modules:
  0.0 208.9 jit_solution(7893829962433769873)
XLA Ops:
  7.4 1.4 scatter_custom_fusion
  8.8 2.0 gather_fusion
  13.5 2.4 %fusion.35 = f32[256,256]{1,0:T(8,128)} fusion(bf16[2048,256]{1,0:T(8,128)(2,1)} %param.14, bf16[256,2048]{1,0:T(8,128)(2,1)S(1)} %gather_fusion.1, pred[256]{0:T(512)(128)(4,1)S(1)} %get-tuple-element.8), kind=kOutput, calls=%fused_computation.61 | convolution fusion | flops 268959744 | bytes 2359552 | tf_op jit(solution)/shard_map/dot_general | solution.py:77
  15.9 7.1 %fusion.37 = f32[256,2048]{1,0:T(8,128)} fusion(bf16[2048,2048]{1,0:T(8,128)(2,1)} %param.12, bf16[256,2048]{1,0:T(8,128)(2,1)S(1)} %gather_fusion.1, pred[256]{0:T(512)(128)(4,1)S(1)} %get-tuple-element.8), kind=kOutput, calls=%fused_computation.63 | convolution fusion | flops 2148007936 | bytes 11534592 | tf_op jit(solution)/shard_map/dot_general | solution.py:75
  23.5 8.4 %psum.7 = f32[256]{0:T(256)S(1)} all-reduce(f32[256]{0:T(256)S(1)} %multiply_reduce_fusion), channel_id=1, replica_groups=mesh['groups'=2,'gx'=4,'gy'=4] {'gx'}, use_global_device_ids=true, to_apply=%region_3.4 | all-reduce | flops 256 | bytes 2048 | tf_op jit(solution)/shard_map/psum | solution.py:78
  32.2 4.1 %reduce-scatter.7.cloned.1.call-done = f32[64,256]{1,0:T(8,128)} async-done(((f32[256,256]{1,0:T(8,128)}), f32[64,256]{1,0:T(8,128)}) %reduce-scatter.7.cloned.1.call-update) | async-done | bytes 65552 | tf_op jit(solution)/shard_map/reduce_scatter | solution.py:81
  36.3 22.7 %reduce-scatter.9.cloned.1.call-done = f32[64,256]{1,0:T(8,128)} async-done(((f32[256,256]{1,0:T(8,128)}), f32[64,256]{1,0:T(8,128)}) %reduce-scatter.9.cloned.1.call-update) | async-done | bytes 65552 | tf_op jit(solution)/shard_map/reduce_scatter | solution.py:82
  59.0 1.6 multiply_convert_fusion.1
  60.5 4.6 %all-to-all-start.1 = ((bf16[4,16,256]{2,1,0:T(8,128)(2,1)}), bf16[4,16,256]{2,1,0:T(8,128)(2,1)S(1)}, u32[]{:S(2)}, u32[]{:S(2)}) async-start(bf16[4,16,256]{2,1,0:T(8,128)(2,1)} %bitcast.4), calls=%async_computation.3 | async-start | bytes 65536 | tf_op jit(solution)/shard_map/all_to_all | solution.py:94
  65.2 5.6 %all-to-all-done.1 = bf16[4,16,256]{2,1,0:T(8,128)(2,1)S(1)} async-done(((bf16[4,16,256]{2,1,0:T(8,128)(2,1)}), bf16[4,16,256]{2,1,0:T(8,128)(2,1)S(1)}, u32[]{:S(2)}, u32[]{:S(2)}) %all-to-all-start.1) | async-done | bytes 32800 | tf_op jit(solution)/shard_map/all_to_all | solution.py:94
  70.8 3.3 %all-to-all-start.2 = ((bf16[4,16,256]{2,1,0:T(8,128)(2,1)}), bf16[4,16,256]{2,1,0:T(8,128)(2,1)S(1)}, u32[]{:S(2)}, u32[]{:S(2)}) async-start(bf16[4,16,256]{2,1,0:T(8,128)(2,1)} %bitcast.9), calls=%async_computation.5 | async-start | bytes 65536 | tf_op jit(solution)/shard_map/all_to_all | solution.py:95
  74.1 18.9 %reduce-scatter.5.cloned.1.call-done = f32[64,2048]{1,0:T(8,128)} async-done(((f32[256,2048]{1,0:T(8,128)}), f32[64,2048]{1,0:T(8,128)}) %reduce-scatter.5.cloned.1.call-update) | async-done | bytes 524304 | tf_op jit(solution)/shard_map/reduce_scatter | solution.py:80
  93.0 1.8 multiply_convert_fusion
  94.8 4.6 %all-to-all-start = ((bf16[4,16,2048]{2,1,0:T(8,128)(2,1)}), bf16[4,16,2048]{2,1,0:T(8,128)(2,1)S(1)}, u32[]{:S(2)}, u32[]{:S(2)}) async-start(bf16[4,16,2048]{2,1,0:T(8,128)(2,1)} %bitcast), calls=%async_computation.1 | async-start | bytes 524288 | tf_op jit(solution)/shard_map/all_to_all | solution.py:93
  99.8 8.5 %all-to-all-done = bf16[4,16,2048]{2,1,0:T(8,128)(2,1)S(1)} async-done(((bf16[4,16,2048]{2,1,0:T(8,128)(2,1)}), bf16[4,16,2048]{2,1,0:T(8,128)(2,1)S(1)}, u32[]{:S(2)}, u32[]{:S(2)}) %all-to-all-start) | async-done | bytes 262176 | tf_op jit(solution)/shard_map/all_to_all | solution.py:93
  109.6 6.5 %select_reduce_fusion = (f32[16,8,8]{2,1,0:T(8,128)S(1)}, f32[16,8,8,192]{3,2,1,0:T(8,128)S(1)}) fusion(pred[16,192]{1,0:T(8,128)(4,1)S(1)} %iota_compare_fusion, bf16[16,8,8,64]{3,2,1,0:T(8,128)(2,1)S(1)} %get-tuple-element.10, bf16[16,8,8,64]{3,2,1,0:T(8,128)(2,1)S(1)} %get-tuple-element.9, bf16[16,192,1024]{2,1,0:T(8,128)(2,1)} %param.16), kind=kOutput, calls=%fused_computation.15 | convolution fusion | flops 51444736 | bytes 7347200 | tf_op jit(solution)/shard_map/rkgd,rckd->rkgc/dot_general | solution.py:48
  116.7 2.0 fusion.15
  118.9 10.9 %all_to_all.58 = bf16[16,4,2048]{2,0,1:T(8,128)(2,1)} all-to-all(bf16[16,4,2048]{2,0,1:T(8,128)(2,1)S(1)} %copy.23), channel_id=1, replica_groups=mesh['groups'=2,'gx'=4,'gy'=4] {'gy'}, dimensions={1} | all-to-all | bytes 524288 | tf_op jit(solution)/shard_map/all_to_all | solution.py:101
  130.1 14.5 %all-gather.2.cloned.1.call-done = bf16[256,2048]{1,0:T(8,128)(2,1)} async-done(((bf16[64,2048]{1,0:T(8,128)(2,1)}), bf16[256,2048]{1,0:T(8,128)(2,1)}) %all-gather.2.cloned.1.call-update) | async-done | bytes 1048592 | tf_op jit(solution)/shard_map/all_gather | solution.py:103
  144.6 6.0 %fusion.39 = f32[256,2048]{1,0:T(8,128)S(1)} fusion(bf16[256,2048]{1,0:T(8,128)(2,1)} %all-gather.2.cloned.1.call-done, bf16[2048,2048]{1,0:T(8,128)(2,1)} %param.15), kind=kOutput, calls=%fused_computation.65 | convolution fusion | flops 2147483648 | bytes 11534336 | tf_op jit(solution)/shard_map/dot_general | solution.py:102
  150.7 2.7 %gather_fusion.2 = f32[256,2048]{1,0:T(8,128)} fusion(f32[256,2048]{1,0:T(8,128)S(1)} %fusion.39, s32[1024]{0:T(1024)S(1)} %pad_clamp_fusion), kind=kCustom, calls=%fused_computation.2 | custom fusion | bytes 4195328 | tf_op jit(solution)/shard_map/jit(_take)/gather | solution.py:107
  153.4 3.1 %broadcast_select_fusion = f32[256,2048]{1,0:T(8,128)} fusion(f32[256,2048]{1,0:T(8,128)} %gather_fusion.2, pred[256]{0:T(512)(128)(4,1)S(1)} %compare_and_fusion.1), kind=kLoop, calls=%fused_computation.13 | loop fusion | flops 524288 | bytes 4194560 | tf_op jit(solution)/shard_map/jit(_take)/select_n | solution.py:107
  156.5 44.0 %reduce-scatter.11.cloned.1.call-done = f32[64,2048]{1,0:T(8,128)} async-done(((f32[256,2048]{1,0:T(8,128)}), f32[64,2048]{1,0:T(8,128)}) %reduce-scatter.11.cloned.1.call-update) | async-done | bytes 524304 | tf_op jit(solution)/shard_map/reduce_scatter | solution.py:108
  200.6 1.8 convert_element_type.84
  (56 shorter events, 6.9 us)
Async XLA Ops:
  6.5 4.3 %copy-start = (bf16[256,2048]{1,0:T(8,128)(2,1)S(1)}, bf16[256,2048]{1,0:T(8,128)(2,1)}, u32[]{:S(2)}) copy-start(bf16[256,2048]{1,0:T(8,128)(2,1)} %param.9) | copy-start | bytes 3145732
  6.5 5.6 %copy-start.2 = (bf16[2048,256]{1,0:T(8,128)(2,1)S(1)}, bf16[2048,256]{1,0:T(8,128)(2,1)}, u32[]{:S(2)}) copy-start(bf16[2048,256]{1,0:T(8,128)(2,1)} %param.13) | copy-start | bytes 3145732
  6.5 29.8 %reduce-scatter.7.cloned.1.call-start = ((), (), s32[]{:S(2)}) async-start(), calls=%async_computation.9 | async-start | bytes 327680 | tf_op jit(solution)/shard_map/reduce_scatter | solution.py:81
  13.4 45.6 %reduce-scatter.9.cloned.1.call-start = ((), (), s32[]{:S(2)}) async-start(), calls=%async_computation.10 | async-start | bytes 327680 | tf_op jit(solution)/shard_map/reduce_scatter | solution.py:82
  15.9 77.1 %reduce-scatter.5.cloned.1.call-start = ((), (), s32[]{:S(2)}) async-start(), calls=%async_computation.8 | async-start | bytes 2621440 | tf_op jit(solution)/shard_map/reduce_scatter | solution.py:80
  60.5 10.3 %all-to-all-start.1 = ((bf16[4,16,256]{2,1,0:T(8,128)(2,1)}), bf16[4,16,256]{2,1,0:T(8,128)(2,1)S(1)}, u32[]{:S(2)}, u32[]{:S(2)}) async-start(bf16[4,16,256]{2,1,0:T(8,128)(2,1)} %bitcast.4), calls=%async_computation.3 | async-start | bytes 65536 | tf_op jit(solution)/shard_map/all_to_all | solution.py:94
  70.8 24.0 %all-to-all-start.2 = ((bf16[4,16,256]{2,1,0:T(8,128)(2,1)}), bf16[4,16,256]{2,1,0:T(8,128)(2,1)S(1)}, u32[]{:S(2)}, u32[]{:S(2)}) async-start(bf16[4,16,256]{2,1,0:T(8,128)(2,1)} %bitcast.9), calls=%async_computation.5 | async-start | bytes 65536 | tf_op jit(solution)/shard_map/all_to_all | solution.py:95
  94.8 13.5 %all-to-all-start = ((bf16[4,16,2048]{2,1,0:T(8,128)(2,1)}), bf16[4,16,2048]{2,1,0:T(8,128)(2,1)S(1)}, u32[]{:S(2)}, u32[]{:S(2)}) async-start(bf16[4,16,2048]{2,1,0:T(8,128)(2,1)} %bitcast), calls=%async_computation.1 | async-start | bytes 524288 | tf_op jit(solution)/shard_map/all_to_all | solution.py:93
  99.4 45.2 %all-gather.2.cloned.1.call-start = ((), (), s32[]{:S(2)}) async-start(), calls=%async_computation.11 | async-start | bytes 1310720 | tf_op jit(solution)/shard_map/all_gather | solution.py:103
  109.0 7.7 %slice-start = ((s8[6291456]{0:T(1024)(128)(4,1)}), s8[4194304]{0:T(1024)(128)(4,1)S(1)}, s32[]{:S(2)}) async-start(s8[6291456]{0:T(1024)(128)(4,1)} %bitcast.54), calls=%async_computation.13 | async-start | bytes 8388608
  109.6 7.1 %slice-start.1 = ((s8[6291456]{0:T(1024)(128)(4,1)}), s8[2097152]{0:T(1024)(128)(4,1)S(1)}, s32[]{:S(2)}) async-start(s8[6291456]{0:T(1024)(128)(4,1)} %bitcast.54), calls=%async_computation.14 | async-start | bytes 4194304
  116.6 13.5 %copy-start.1 = (s32[256]{0:T(256)S(1)}, s32[256]{0:T(256)}, u32[]{:S(2)}) copy-start(s32[256]{0:T(256)} %param.10) | copy-start | bytes 3076
  129.8 70.7 %reduce-scatter.11.cloned.1.call-start = ((), (), s32[]{:S(2)}) async-start(), calls=%async_computation.12 | async-start | bytes 2621440 | tf_op jit(solution)/shard_map/reduce_scatter | solution.py:108
Sparse Core Ops, SparseCore 0:
  13.5 22.7 reduce-scatter.6
  38.9 20.0 reduce-scatter.8
  61.5 31.4 reduce-scatter.4
  129.9 14.6 all-gather.1
  156.7 43.8 reduce-scatter.10
where the time goes:
time: 210 us; the launch traced here: 209 us
  waiting for transfers between devices  118 us (56%)
  matrix products  25.6 us (12%)
  blocking collectives  19.3 us (9%)
  between operations  13.4 us (6%)
  starting transfers between devices  12.8 us (6%)
  other arithmetic  10.9 us (5%)
  local copies, waits for them, and re-layouts  8.44 us (4%)
    reduce_scatter x1, waiting for transfers between devices, body(): mixed = lax.psum_scatter(by_request, 'gy', scatter_dimension=0, tiled=True)  44 us
    reduce_scatter x1, waiting for transfers between devices, body(): lax.psum_scatter(value_part, 'gx', scatter_dimension=0, tiled=True)  22.7 us
    reduce_scatter x1, waiting for transfers between devices, body(): lax.psum_scatter(query_part, 'gx', scatter_dimension=0, tiled=True)  18.9 us
    all_gather x1, waiting for transfers between devices, body(): lax.all_gather(returned, 'gx', axis=0, tiled=True)  14.5 us
    all_to_all x1, blocking collectives, body(): lax.all_to_all(attn, 'gy', split_axis=1, concat_axis=0, tiled=True)  10.9 us
    all_to_all x1, waiting for transfers between devices, body(): lax.all_to_all(query, 'gy', split_axis=0, concat_axis=1, tiled=True)  8.54 us
    psum x1, blocking collectives, body(): square_sums = lax.psum(squares, 'gx')  8.37 us
    dot_general x1, matrix products, body(): query_part = jnp.dot(ordered, w_query, preferred_element_type=jnp.float32)  7.13 us
  transfers between devices with their start and end apart: 8, of which 7 were waited for; matrix products, arithmetic and copies ran while one was open for 7% of the time, Pallas kernels for 0%

commit v1 on v0

v1 whole, which is shorter than its diff:
```python
import functools
import math

import jax
import jax.numpy as jnp
from jax import lax
from jax.experimental import pallas as pl
from jax.experimental.pallas import tpu as pltpu
from jax.sharding import PartitionSpec as P

D = 8192
H = 64
KVH = 8
HD = 128
EPS = 1e-05
THETA = 500000.0
MESH = pl.DeviceIdType.MESH
F32 = jnp.float32
BF16 = jnp.bfloat16
NCH = 5
NOUT = 4
PAD = 16


def kernel(
    gxn, gyn,
    hidden, crow_lane, crow_col, cos2, sin2, bias,
    w_query, w_key, w_value, w_output, k_cache, v_cache,
    out,
    wbuf, wobuf, kbuf, vbuf, ordered, sq, own, xsend, xrecv, sqrecv, ysend, yrecv, mine,
    sqysend, sqyrecv, inv, fin, qrecv, qs, os, asend, gath, perm, fsend, frecv, facc,
    w_sem, wo_sem, kv_sem, xs, xr, ys, yr, qsem, qr, asem, ar, es, er, cs, cr, fs, fr,
):
    gx = lax.axis_index("gx")
    gy = lax.axis_index("gy")
    ny = gxn // 2
    y = gx // 2
    core = gx % 2
    partner = y * 2 + (1 - core)
    ctx = k_cache.shape[1]
    rl = k_cache.shape[0]
    blk = ordered.shape[1]
    requests = blk * gxn
    hl = H // gyn
    kvl = KVH // gyn
    group = H // KVH
    cw = wbuf.shape[2]
    half = cw // 2
    ow = wobuf.shape[2]

    def ypeer(j):
        return lax.rem(y + j, ny)

    def zpeer(k):
        return lax.rem(gy + k, gyn)

    w_copies = [
        [pltpu.make_async_copy(w_query.at[:, pl.ds(c * cw, cw)], wbuf.at[c], w_sem.at[c])]
        for c in range(NCH - 1)
    ]
    w_copies.append([
        pltpu.make_async_copy(w_key, wbuf.at[NCH - 1, :, pl.ds(0, half)], w_sem.at[NCH - 1]),
        pltpu.make_async_copy(w_value, wbuf.at[NCH - 1, :, pl.ds(half, half)], w_sem.at[NCH]),
    ])
    order = [NCH - 1] + list(range(NCH - 1))
    for c in order:
        for copy in w_copies[c]:
            copy.start()
    kv_copies = [
        pltpu.make_async_copy(k_cache, kbuf.at[:, pl.ds(0, ctx), :], kv_sem.at[0]),
        pltpu.make_async_copy(v_cache, vbuf.at[:, pl.ds(0, ctx), :], kv_sem.at[1]),
    ]
    wo_copies = [
        pltpu.make_async_copy(w_output.at[:, pl.ds(n * ow, ow)], wobuf.at[n], wo_sem.at[n])
        for n in range(NOUT)
    ]

    barrier = pltpu.get_barrier_semaphore()
    pl.semaphore_signal(barrier, inc=1, device_id={"gx": partner}, device_id_type=MESH)
    for j in range(1, ny):
        pl.semaphore_signal(
            barrier, inc=1, device_id={"gx": ypeer(j) * 2 + core}, device_id_type=MESH
        )
    for k in range(1, gyn):
        pl.semaphore_signal(barrier, inc=1, device_id={"gy": zpeer(k)}, device_id_type=MESH)

    def reorder(b, carry):
        parity = jnp.where(b < ny, 1 - core, core)
        source = lax.rem(y + lax.rem(b, ny), ny) * 2 + parity
        wanted = lax.broadcasted_iota(jnp.int32, (blk, requests), 0) + source * blk
        chosen = jnp.where(crow_lane[...] == wanted, 1.0, 0.0).astype(BF16)
        rows = jnp.dot(chosen, hidden[...], preferred_element_type=F32)
        ordered[b] = rows.astype(BF16)
        sq[b] = jnp.broadcast_to(jnp.sum(rows * rows, axis=1, keepdims=True), (blk, HD))
        return carry

    lax.fori_loop(0, gxn, reorder, 0)
    pl.semaphore_wait(barrier, 1 + (ny - 1) + (gyn - 1))

    def remote(src, dst, send, recv, **where):
        return pltpu.make_async_remote_copy(
            src_ref=src, dst_ref=dst, send_sem=send, recv_sem=recv,
            device_id=where, device_id_type=MESH,
        )

    def x_copy(c):
        return remote(xsend.at[c], xrecv.at[c], xs.at[c], xr.at[c], gx=partner)

    def y_copy(c, j):
        return remote(
            ysend.at[c, j], yrecv.at[c, j], ys.at[c, j], yr.at[c, j], gx=ypeer(j) * 2 + core
        )

    sq_x = remote(sq.at[pl.ds(0, ny)], sqrecv, xs.at[NCH], xr.at[NCH], gx=partner)

    def sq_y(j):
        return remote(
            sqysend.at[j], sqyrecv.at[j], ys.at[NCH, j], yr.at[NCH, j], gx=ypeer(j) * 2 + core
        )

    def q_copy(c, k):
        peer = zpeer(k)
        return remote(
            fin.at[c, peer], qrecv.at[gy, c], qsem.at[c, k], qr.at[gy, c], gy=peer
        )

    def stage1(c):
        for copy in w_copies[c]:
            copy.wait()
        rows = ordered[...].reshape(requests, ordered.shape[2])
        part = jnp.dot(rows, wbuf[c], preferred_element_type=F32)
        xsend[c] = part[: requests // 2].astype(BF16)
        x_copy(c).start()
        own[c] = part[requests // 2 :]

    def stage2(c):
        x_copy(c).wait_recv()
        for j in range(1, ny):
            rows = pl.ds(j * blk, blk)
            ysend[c, j] = (own[c, rows, :] + xrecv[c, rows, :].astype(F32)).astype(BF16)
            y_copy(c, j).start()
        rows = pl.ds(0, blk)
        mine[c] = own[c, rows, :] + xrecv[c, rows, :].astype(F32)

    def stage3(c):
        total = mine[c]
        for j in range(1, ny):
            y_copy(c, j).wait_recv()
            total = total + yrecv[c, j].astype(F32)
        scaled = (total * inv[...]).astype(BF16)
        for k in range(gyn):
            fin[c, k] = scaled[k * rl : (k + 1) * rl]
        for k in range(1, gyn):
            q_copy(c, k).start()
        qrecv[gy, c] = fin[c, gy]

    sq_x.start()
    for step in range(NCH + 2):
        if step < NCH:
            stage1(order[step])
        if step == 1:
            for copy in kv_copies:
                copy.start()
            sq_x.wait_recv()
            for j in range(1, ny):
                sqysend[j] = sq[ny + j] + sqrecv[j]
                sq_y(j).start()
        if 1 <= step <= NCH:
            stage2(order[step - 1])
        if step == 2:
            total = sq[ny] + sqrecv[0]
            for j in range(1, ny):
                sq_y(j).wait_recv()
                total = total + sqyrecv[j]
            inv[...] = lax.rsqrt(total[:, :1] / D + EPS)
        if step >= 2:
            stage3(order[step - 2])
    for copy in wo_copies:
        copy.start()
    for copy in kv_copies:
        copy.wait()

    cosine = cos2[...]
    sine = sin2[...]
    scale = 1.0 / math.sqrt(HD)
    first_row = lax.broadcasted_iota(jnp.int32, (PAD, HD), 0) == 0
    head = lax.broadcasted_iota(jnp.int32, (hl, HD), 0) // group

    def turned(values):
        values = values.astype(F32)
        return values * cosine + pltpu.roll(values, HD // 2, 1) * sine

    def a_copy(k):
        peer = zpeer(k)
        return remote(asend.at[peer], gath.at[gx, gy], asem.at[k], ar.at[gy], gy=peer)

    def attention(k, carry):
        source = zpeer(k)

        @pl.when(k > 0)
        def _():
            for c in order:
                remote(
                    fin.at[c, source], qrecv.at[source, c], qsem.at[c, k], qr.at[source, c],
                    gy=source,
                ).wait_recv()

        for h in range(hl):
            at = h * HD
            q = qrecv[source, at // cw, :, at % cw : at % cw + HD]
            qs[:, h, :] = turned(q).astype(BF16).astype(F32)
        for g in range(kvl):
            key = turned(qrecv[source, NCH - 1, :, g * HD : (g + 1) * HD])
            value = qrecv[source, NCH - 1, :, half + g * HD : half + (g + 1) * HD].astype(F32)
            columns = pl.ds(pl.multiple_of((source * kvl + g) * HD, HD), HD)
            for r in range(rl):
                kbuf[r, pl.ds(ctx, PAD), columns] = jnp.where(
                    first_row, key[r : r + 1], 0.0
                ).astype(BF16)
                vbuf[r, pl.ds(ctx, PAD), columns] = jnp.where(
                    first_row, value[r : r + 1], 0.0
                ).astype(BF16)
        columns = pl.ds(pl.multiple_of(source * kvl * HD, kvl * HD), kvl * HD)
        scores = []
        for r in range(rl):
            q = qs[r]
            wide = jnp.concatenate(
                [jnp.where(head == g, q, 0.0) for g in range(kvl)], axis=1
            ).astype(BF16)
            scores.append(
                lax.dot_general(
                    wide, kbuf[r, :, columns], (((1,), (1,)), ((), ())),
                    preferred_element_type=F32,
                ) * scale + bias[r : r + 1]
            )
        for r in range(rl):
            highest = jnp.max(scores[r], axis=1, keepdims=True)
            weights = jnp.exp(scores[r] - highest)
            denominator = jnp.sum(weights, axis=1, keepdims=True)
            wide = jnp.dot(
                weights.astype(BF16), vbuf[r, :, columns], preferred_element_type=F32
            )
            picked = wide[:, :HD]
            for g in range(1, kvl):
                picked = jnp.where(head == g, wide[:, g * HD : (g + 1) * HD], picked)
            os[r] = picked / denominator
        for h in range(hl):
            asend[source, :, h * HD : (h + 1) * HD] = os[:, h, :].astype(BF16)

        @pl.when(k > 0)
        def _():
            a_copy(k).start()

        @pl.when(k == 0)
        def _():
            gath[gx, gy] = asend[gy]

        return carry

    lax.fori_loop(0, gyn, attention, 0)

    def e_copy(row, piece, j):
        return remote(
            gath.at[row, piece], gath.at[row, piece], es.at[j, piece], er.at[row // 2, piece],
            gx=ypeer(j) * 2 + core,
        )

    def c_copy(row, piece):
        return remote(
            gath.at[row, piece], gath.at[row, piece], cs.at[row // 2, piece],
            cr.at[row // 2, piece], gx=partner,
        )

    for k in range(gyn):
        piece = zpeer(k)
        if k > 0:
            remote(
                asend.at[piece], gath.at[gx, piece], asem.at[k], ar.at[piece], gy=piece
            ).wait_recv()
        for j in range(1, ny):
            e_copy(gx, piece, j).start()
        c_copy(gx, piece).start()
    for k in range(gyn):
        piece = zpeer(k)
        for j in range(1, ny):
            row = ypeer(j) * 2 + core
            e_copy(row, piece, j).wait_recv()
            c_copy(row, piece).start()
    for k in range(gyn):
        piece = zpeer(k)
        for j in range(ny):
            c_copy(ypeer(j) * 2 + 1 - core, piece).wait_recv()

    zblk = perm.shape[1]

    def permute(k, carry):
        wanted = crow_col[zpeer(k)]
        lanes = lax.broadcasted_iota(jnp.int32, (zblk, requests), 1)
        chosen = jnp.where(wanted == lanes, 1.0, 0.0).astype(BF16)
        rows = gath[...].reshape(requests, hl * HD)
        perm[k] = jnp.dot(chosen, rows, preferred_element_type=F32).astype(BF16)
        return carry

    lax.fori_loop(0, gyn, permute, 0)

    def f_copy(n, k):
        return remote(fsend.at[n, k], frecv.at[n, k], fs.at[n, k], fr.at[n, k], gy=zpeer(k))

    for n in range(NOUT):
        wo_copies[n].wait()
        rows = perm[...].reshape(requests, hl * HD)
        part = jnp.dot(rows, wobuf[n], preferred_element_type=F32)
        for k in range(1, gyn):
            fsend[n, k] = part[k * zblk : (k + 1) * zblk].astype(BF16)
            f_copy(n, k).start()
        facc[n] = part[:zblk]
    for n in range(NOUT):
        total = facc[n]
        for k in range(1, gyn):
            f_copy(n, k).wait_recv()
            total = total + frecv[n, k].astype(F32)
        out[:, n * ow : (n + 1) * ow] = total.astype(BF16)

    sq_x.wait_send()
    for j in range(1, ny):
        sq_y(j).wait_send()
    for c in range(NCH):
        x_copy(c).wait_send()
        for j in range(1, ny):
            y_copy(c, j).wait_send()
        for k in range(1, gyn):
            q_copy(c, k).wait_send()
    for k in range(1, gyn):
        a_copy(k).wait_send()
    for k in range(gyn):
        piece = zpeer(k)
        for j in range(1, ny):
            e_copy(gx, piece, j).wait_send()
        for j in range(ny):
            c_copy(ypeer(j) * 2 + core, piece).wait_send()
    for n in range(NOUT):
        for k in range(1, gyn):
            f_copy(n, k).wait_send()


def body(gxn, gyn, hidden, cache_row, ctx_len, w_query, w_key, w_value, w_output, k_cache, v_cache):
    requests = cache_row.shape[0]
    rl, ctx, width = k_cache.shape
    ny = gxn // 2
    blk = requests // gxn
    zblk = requests // gyn
    dl = hidden.shape[1]
    hl = H // gyn
    cols = w_query.shape[1] + w_key.shape[1] + w_value.shape[1]
    cw = cols // NCH
    outw = w_output.shape[1]
    ow = outw // NOUT

    first = (lax.axis_index("gx") * gyn + lax.axis_index("gy")) * rl
    rows = first + jnp.arange(rl, dtype=jnp.int32)
    lengths = jnp.sum(
        jnp.where(cache_row[None, :] == rows[:, None], ctx_len[None, :], 0), axis=1
    )
    freq = jnp.exp(jnp.arange(HD // 2, dtype=F32) * (-2.0 * math.log(THETA) / HD))
    angle = lengths.astype(F32)[:, None] * freq[None, :]
    cosine = jnp.cos(angle)
    sine = jnp.sin(angle)
    cos2 = jnp.concatenate([cosine, cosine], axis=1)
    sin2 = jnp.concatenate([-sine, sine], axis=1)
    slot = jnp.arange(ctx + PAD, dtype=jnp.int32)[None, :]
    bias = jnp.where((slot < lengths[:, None]) & (slot < ctx) | (slot == ctx), 0.0, -jnp.inf)

    vm = pl.BlockSpec(memory_space=pltpu.VMEM)
    hbm = pl.BlockSpec(memory_space=pl.ANY)
    dma = pltpu.SemaphoreType.DMA
    V = pltpu.VMEM
    return pl.pallas_call(
        functools.partial(kernel, gxn, gyn),
        out_shape=jax.ShapeDtypeStruct((zblk, outw), BF16),
        in_specs=[vm] * 6 + [hbm] * 6,
        out_specs=vm,
        scratch_shapes=[
            V((NCH, dl, cw), BF16),
            V((NOUT, hl * HD, ow), BF16),
            V((rl, ctx + PAD, width), BF16),
            V((rl, ctx + PAD, width), BF16),
            V((gxn, blk, dl), BF16),
            V((gxn, blk, HD), F32),
            V((NCH, requests // 2, cw), F32),
            V((NCH, requests // 2, cw), BF16),
            V((NCH, requests // 2, cw), BF16),
            V((ny, blk, HD), F32),
            V((NCH, ny, blk, cw), BF16),
            V((NCH, ny, blk, cw), BF16),
            V((NCH, blk, cw), F32),
            V((ny, blk, HD), F32),
            V((ny, blk, HD), F32),
            V((blk, 1), F32),
            V((NCH, gyn, rl, cw), BF16),
            V((gyn, NCH, rl, cw), BF16),
            V((rl, hl, HD), F32),
            V((rl, hl, HD), F32),
            V((gyn, rl, hl * HD), BF16),
            V((gxn, gyn, rl, hl * HD), BF16),
            V((gyn, zblk, hl * HD), BF16),
            V((NOUT, gyn, zblk, ow), BF16),
            V((NOUT, gyn, zblk, ow), BF16),
            V((NOUT, zblk, ow), F32),
            dma((NCH + 1,)), dma((NOUT,)), dma((2,)),
            dma((NCH + 1,)), dma((NCH + 1,)),
            dma((NCH + 1, ny)), dma((NCH + 1, ny)),
            dma((NCH, gyn)), dma((gyn, NCH)),
            dma((gyn,)), dma((gyn,)),
            dma((ny, gyn)), dma((ny, gyn)),
            dma((ny, gyn)), dma((ny, gyn)),
            dma((NOUT, gyn)), dma((NOUT, gyn)),
        ],
        compiler_params=pltpu.CompilerParams(
            collective_id=0, has_side_effects=True, vmem_limit_bytes=60 * 1024 * 1024
        ),
        cost_estimate=pl.CostEstimate(
            flops=2 * requests * dl * cols, bytes_accessed=2 * dl * cols, transcendentals=0
        ),
    )(
        hidden, cache_row[None, :], cache_row.reshape(gyn, zblk, 1), cos2, sin2, bias,
        w_query, w_key, w_value, w_output, k_cache, v_cache,
    )


def solution(mesh):
    placed = (
        P("groups", "gx"),
        P("groups"),
        P("groups"),
        P("gx", "gy"),
        P("gx", "gy"),
        P("gx", "gy"),
        P("gy", "gx"),
        P(("groups", "gx", "gy"), None, None),
        P(("groups", "gx", "gy"), None, None),
    )
    return jax.shard_map(
        functools.partial(body, mesh.shape["gx"], mesh.shape["gy"]),
        mesh=mesh, in_specs=placed, out_specs=P(("groups", "gy"), "gx"), check_vma=False,
    )
```

time: 210 us -> 69.6 us (0.33)
  waiting for transfers between devices: 118 us -> 0 us
  Pallas kernels: 0 us -> 63.5 us
  matrix products: 25.6 us -> 0 us
  blocking collectives: 19.3 us -> 0 us
  between operations: 13.4 us -> 0.03 us
  starting transfers between devices: 12.8 us -> 0 us
  other arithmetic: 10.9 us -> 2.37 us
  local copies, waits for them, and re-layouts: 8.44 us -> 3.21 us
    reduce_scatter x4 -> x0, waiting for transfers between devices: 89.7 us -> none  [the longest x1 44 us: body(): mixed = lax.psum_scatter(by_request, 'gy', scatter_dimension=0, tiled=True)]
    pallas_call x0 -> x1, Pallas kernels: none -> 63.5 us  [body(): pl.pallas_call(functools.partial(kernel, gxn, gyn), out_shape=jax.ShapeDt...]
    dot_general x7 -> x0, matrix products: 25.6 us -> none  [the longest x1 7.13 us: body(): query_part = jnp.dot(ordered, w_query, preferred_element_type=jnp.float32)]
    all_gather x1 -> x0, waiting for transfers between devices: 14.5 us -> none  [body(): lax.all_gather(returned, 'gx', axis=0, tiled=True)]
    all_to_all x3 -> x0, waiting for transfers between devices: 14.1 us -> none  [the longest x1 8.54 us: body(): lax.all_to_all(query, 'gy', split_axis=0, concat_axis=1, tiled=True)]
    all_to_all x3 -> x0, starting transfers between devices: 12.5 us -> none  [the longest x1 4.6 us: body(): lax.all_to_all(query, 'gy', split_axis=0, concat_axis=1, tiled=True)]
    all_to_all x1 -> x0, blocking collectives: 10.9 us -> none  [body(): lax.all_to_all(attn, 'gy', split_axis=1, concat_axis=0, tiled=True)]
    psum x1 -> x0, blocking collectives: 8.37 us -> none  [body(): square_sums = lax.psum(squares, 'gx')]
  transfers between devices with their start and end apart: 8 -> 0, of which waited for: 7 -> 0; matrix products, arithmetic and copies ran while one was open for 7% -> 0% of each run, Pallas kernels for 0% -> 0%
where the time goes in v1:
time: 69.6 us; the launch traced here: 69.1 us
  Pallas kernels  63.5 us (91%)
  local copies, waits for them, and re-layouts  3.21 us (5%)
  other arithmetic  2.37 us (3%)
    pallas_call x1, Pallas kernels, body(): pl.pallas_call(functools.partial(kernel, gxn, gyn), out_shape=jax.ShapeDt...  63.5 us
    unnamed x1, local copies, waits for them, and re-layouts  1.67 us
    reshape x1, local copies, waits for them, and re-layouts, body(): cache_row.reshape(gyn, zblk, 1)  1.54 us

profile of v1, /device:TPU:0, one launch (start us, length us, event | category | flops | bytes accessed | tf_op | source)
XLA Modules:
  0.0 69.1 jit_solution(12056570711104078327)
XLA Ops:
  0.0 0.9 %select_reduce_fusion = s32[16]{0:T(128)S(1)} fusion(s32[256]{0:T(256)} %param.11, s32[256]{0:T(256)} %param.10, s32[16]{0:T(128)S(1)} %iota_add_fusion), kind=kLoop, calls=%fused_computation.1 | loop fusion | flops 12272 | bytes 2176 | tf_op jit(solution)/shard_map/reduce_sum | solution.py:361
  0.9 0.7 fusion.2.bias
  1.6 0.1 fusion.3
  1.7 0.7 pad_maximum_fusion
  2.4 1.5 %reshape.29.crow_col = s32[4,64,1]{2,1,0:T(8,128)} reshape(s32[256]{0:T(256)} %param.10) | data formatting | bytes 2048 | tf_op jit(solution)/shard_map/reshape | solution.py:425
  3.9 63.5 %shard_map.91 = bf16[64,2048]{1,0:T(8,128)(2,1)} custom-call(bf16[256,2048]{1,0:T(8,128)(2,1)} %hidden.1, s32[1,256]{1,0:T(1,128)} %bitcast.1, s32[4,64,1]{2,1,0:T(8,128)} %reshape.29.crow_col, f32[16,128]{1,0:T(8,128)} %get-tuple-element.8.cos2, f32[16,128]{1,0:T(8,128)} %get-tuple-element.9.sin2, f32[16,208]{1,0:T(8,128)} %fusion.2.bias, ...), custom_call_target="tpu_custom_call" | custom-call | flops 2684354560 | bytes 10485760 | tf_op jit(solution)/shard_map/pallas_call | solution.py:377
  67.4 1.7 %copy.13 = bf16[64,2048]{1,0:T(8,128)(2,1)} copy(bf16[64,2048]{1,0:T(8,128)(2,1)} %shard_map.91) | data formatting | bytes 524288
  (4 shorter events, 0.0 us)

commit v2 on v1

--- a/solution.py
+++ b/solution.py
@@ -19,17 +19,19 @@
 BF16 = jnp.bfloat16
 NCH = 5
 NOUT = 4
+AHEAD = 2
 PAD = 16
 
 
 def kernel(
     gxn, gyn,
-    hidden, crow_lane, crow_col, cos2, sin2, bias,
+    hidden, crow, clen,
     w_query, w_key, w_value, w_output, k_cache, v_cache,
     out,
-    wbuf, wobuf, kbuf, vbuf, ordered, sq, own, xsend, xrecv, sqrecv, ysend, yrecv, mine,
-    sqysend, sqyrecv, inv, fin, qrecv, qs, os, asend, gath, perm, fsend, frecv, facc,
-    w_sem, wo_sem, kv_sem, xs, xr, ys, yr, qsem, qr, asem, ar, es, er, cs, cr, fs, fr,
+    wbuf, wobuf, kbuf, vbuf, ordered, sq, own, xsend, xrecv, sqrecv, ysend, yrecv,
+    sqysend, sqyrecv, inv, cos2, sin2, bias, fin, qrecv, qs, os, asend, gath, row_of, perm,
+    fsend, frecv, mrecv, facc, fkeep,
+    w_sem, wo_sem, kv_sem, xs, xr, ys, yr, qsem, qr, asem, ar, es, er, cs, cr, fs, fr, ms,
 ):
     gx = lax.axis_index("gx")
     gy = lax.axis_index("gy")
@@ -88,14 +90,15 @@
         parity = jnp.where(b < ny, 1 - core, core)
         source = lax.rem(y + lax.rem(b, ny), ny) * 2 + parity
         wanted = lax.broadcasted_iota(jnp.int32, (blk, requests), 0) + source * blk
-        chosen = jnp.where(crow_lane[...] == wanted, 1.0, 0.0).astype(BF16)
+        chosen = jnp.where(crow[...] == wanted, 1.0, 0.0).astype(BF16)
         rows = jnp.dot(chosen, hidden[...], preferred_element_type=F32)
         ordered[b] = rows.astype(BF16)
         sq[b] = jnp.broadcast_to(jnp.sum(rows * rows, axis=1, keepdims=True), (blk, HD))
         return carry
 
+    for copy in kv_copies + wo_copies:
+        copy.start()
     lax.fori_loop(0, gxn, reorder, 0)
-    pl.semaphore_wait(barrier, 1 + (ny - 1) + (gyn - 1))
 
     def remote(src, dst, send, recv, **where):
         return pltpu.make_async_remote_copy(
@@ -108,7 +111,7 @@
 
     def y_copy(c, j):
         return remote(
-            ysend.at[c, j], yrecv.at[c, j], ys.at[c, j], yr.at[c, j], gx=ypeer(j) * 2 + core
+            ysend.at[c, j - 1], yrecv.at[c, j - 1], ys.at[c, j], yr.at[c, j], gx=ypeer(j) * 2 + core
         )
 
     sq_x = remote(sq.at[pl.ds(0, ny)], sqrecv, xs.at[NCH], xr.at[NCH], gx=partner)
@@ -124,29 +127,28 @@
             fin.at[c, peer], qrecv.at[gy, c], qsem.at[c, k], qr.at[gy, c], gy=peer
         )
 
-    def stage1(c):
+    def product(c):
         for copy in w_copies[c]:
             copy.wait()
         rows = ordered[...].reshape(requests, ordered.shape[2])
         part = jnp.dot(rows, wbuf[c], preferred_element_type=F32)
         xsend[c] = part[: requests // 2].astype(BF16)
-        x_copy(c).start()
         own[c] = part[requests // 2 :]
 
     def stage2(c):
         x_copy(c).wait_recv()
         for j in range(1, ny):
             rows = pl.ds(j * blk, blk)
-            ysend[c, j] = (own[c, rows, :] + xrecv[c, rows, :].astype(F32)).astype(BF16)
+            ysend[c, j - 1] = (own[c, rows, :] + xrecv[c, rows, :].astype(F32)).astype(BF16)
             y_copy(c, j).start()
         rows = pl.ds(0, blk)
-        mine[c] = own[c, rows, :] + xrecv[c, rows, :].astype(F32)
+        own[c, rows, :] = own[c, rows, :] + xrecv[c, rows, :].astype(F32)
 
     def stage3(c):
-        total = mine[c]
+        total = own[c, pl.ds(0, blk), :]
         for j in range(1, ny):
             y_copy(c, j).wait_recv()
-            total = total + yrecv[c, j].astype(F32)
+            total = total + yrecv[c, j - 1].astype(F32)
         scaled = (total * inv[...]).astype(BF16)
         for k in range(gyn):
             fin[c, k] = scaled[k * rl : (k + 1) * rl]
@@ -154,13 +156,40 @@
             q_copy(c, k).start()
         qrecv[gy, c] = fin[c, gy]
 
+    for c in order[:AHEAD]:
+        product(c)
+    first_row = (gx * gyn + gy) * rl
+    wanted = lax.broadcasted_iota(jnp.int32, (rl, requests), 0) + first_row
+    lengths = jnp.sum(
+        jnp.where(crow[...] == wanted, clen[...].astype(F32), 0.0), axis=1, keepdims=True
+    )
+    lane = lax.broadcasted_iota(jnp.int32, (1, HD), 1)
+    pair = lax.rem(lane, HD // 2).astype(F32)
+    angle = lengths * jnp.exp(pair * (-2.0 * math.log(THETA) / HD))
+    cos2[...] = jnp.cos(angle)
+    sine = jnp.sin(angle)
+    sin2[...] = jnp.where(lane < HD // 2, -sine, sine)
+    slot = lax.broadcasted_iota(jnp.int32, (rl, ctx + PAD), 1)
+    bias[...] = jnp.where(
+        (slot == ctx) | ((slot < ctx) & (slot.astype(F32) < lengths)), 0.0, -jnp.inf
+    )
+
+    def select(b, carry):
+        at = pl.ds(pl.multiple_of(b * HD, HD), HD)
+        row_of[at, :] = jnp.broadcast_to(crow[:, at].astype(F32), (HD, HD)).T
+        return carry
+
+    lax.fori_loop(0, requests // HD, select, 0)
+    pl.semaphore_wait(barrier, 1 + (ny - 1) + (gyn - 1))
+
     sq_x.start()
+    for c in order[:AHEAD]:
+        x_copy(c).start()
     for step in range(NCH + 2):
-        if step < NCH:
-            stage1(order[step])
+        if AHEAD <= step < NCH:
+            product(order[step])
+            x_copy(order[step]).start()
         if step == 1:
-            for copy in kv_copies:
-                copy.start()
             sq_x.wait_recv()
             for j in range(1, ny):
                 sqysend[j] = sq[ny + j] + sqrecv[j]
@@ -175,24 +204,34 @@
             inv[...] = lax.rsqrt(total[:, :1] / D + EPS)
         if step >= 2:
             stage3(order[step - 2])
-    for copy in wo_copies:
-        copy.start()
     for copy in kv_copies:
         copy.wait()
 
     cosine = cos2[...]
-    sine = sin2[...]
+    turn = sin2[...]
     scale = 1.0 / math.sqrt(HD)
-    first_row = lax.broadcasted_iota(jnp.int32, (PAD, HD), 0) == 0
+    top = lax.broadcasted_iota(jnp.int32, (PAD, HD), 0) == 0
     head = lax.broadcasted_iota(jnp.int32, (hl, HD), 0) // group
 
     def turned(values):
         values = values.astype(F32)
-        return values * cosine + pltpu.roll(values, HD // 2, 1) * sine
+        return values * cosine + pltpu.roll(values, HD // 2, 1) * turn
 
     def a_copy(k):
         peer = zpeer(k)
         return remote(asend.at[peer], gath.at[gx, gy], asem.at[k], ar.at[gy], gy=peer)
+
+    def e_copy(row, piece, j):
+        return remote(
+            gath.at[row, piece], gath.at[row, piece], es.at[j, piece], er.at[row // 2, piece],
+            gx=ypeer(j) * 2 + core,
+        )
+
+    def c_copy(row, piece):
+        return remote(
+            gath.at[row, piece], gath.at[row, piece], cs.at[row // 2, piece],
+            cr.at[row // 2, piece], gx=partner,
+        )
 
     def attention(k, carry):
         source = zpeer(k)
@@ -215,10 +254,10 @@
             columns = pl.ds(pl.multiple_of((source * kvl + g) * HD, HD), HD)
             for r in range(rl):
                 kbuf[r, pl.ds(ctx, PAD), columns] = jnp.where(
-                    first_row, key[r : r + 1], 0.0
+                    top, key[r : r + 1], 0.0
                 ).astype(BF16)
                 vbuf[r, pl.ds(ctx, PAD), columns] = jnp.where(
-                    first_row, value[r : r + 1], 0.0
+                    top, value[r : r + 1], 0.0
                 ).astype(BF16)
         columns = pl.ds(pl.multiple_of(source * kvl * HD, kvl * HD), kvl * HD)
         scores = []
@@ -231,7 +270,7 @@
                 lax.dot_general(
                     wide, kbuf[r, :, columns], (((1,), (1,)), ((), ())),
                     preferred_element_type=F32,
-                ) * scale + bias[r : r + 1]
+                ) * scale + bias[pl.ds(r, 1), :]
             )
         for r in range(rl):
             highest = jnp.max(scores[r], axis=1, keepdims=True)
@@ -254,71 +293,107 @@
         @pl.when(k == 0)
         def _():
             gath[gx, gy] = asend[gy]
+            for j in range(1, ny):
+                e_copy(gx, gy, j).start()
+            c_copy(gx, gy).start()
 
         return carry
 
     lax.fori_loop(0, gyn, attention, 0)
 
-    def e_copy(row, piece, j):
-        return remote(
-            gath.at[row, piece], gath.at[row, piece], es.at[j, piece], er.at[row // 2, piece],
-            gx=ypeer(j) * 2 + core,
-        )
-
-    def c_copy(row, piece):
-        return remote(
-            gath.at[row, piece], gath.at[row, piece], cs.at[row // 2, piece],
-            cr.at[row // 2, piece], gx=partner,
-        )
-
-    for k in range(gyn):
-        piece = zpeer(k)
-        if k > 0:
-            remote(
-                asend.at[piece], gath.at[gx, piece], asem.at[k], ar.at[piece], gy=piece
-            ).wait_recv()
+    def zback(k):
+        return lax.rem(gy - k + gyn, gyn)
+
+    for k in range(1, gyn):
+        piece = zback(k)
+        remote(
+            asend.at[piece], gath.at[gx, piece], asem.at[k], ar.at[piece], gy=piece
+        ).wait_recv()
         for j in range(1, ny):
             e_copy(gx, piece, j).start()
         c_copy(gx, piece).start()
     for k in range(gyn):
-        piece = zpeer(k)
+        piece = zback(k)
         for j in range(1, ny):
             row = ypeer(j) * 2 + core
             e_copy(row, piece, j).wait_recv()
             c_copy(row, piece).start()
     for k in range(gyn):
-        piece = zpeer(k)
+        piece = zback(k)
         for j in range(ny):
             c_copy(ypeer(j) * 2 + 1 - core, piece).wait_recv()
 
     zblk = perm.shape[1]
-
-    def permute(k, carry):
-        wanted = crow_col[zpeer(k)]
-        lanes = lax.broadcasted_iota(jnp.int32, (zblk, requests), 1)
-        chosen = jnp.where(wanted == lanes, 1.0, 0.0).astype(BF16)
-        rows = gath[...].reshape(requests, hl * HD)
-        perm[k] = jnp.dot(chosen, rows, preferred_element_type=F32).astype(BF16)
-        return carry
-
-    lax.fori_loop(0, gyn, permute, 0)
-
-    def f_copy(n, k):
-        return remote(fsend.at[n, k], frecv.at[n, k], fs.at[n, k], fr.at[n, k], gy=zpeer(k))
+    nh = gyn // 2
+    side = gy // nh
+    place = lax.rem(gy, nh)
+    middle = jnp.where(side == 0, nh - 1 - place, place)
+
+    def at_place(which, m):
+        return jnp.where(which == 0, nh - 1 - m, nh + m)
+
+    def target(t):
+        if t < nh:
+            return at_place(side, lax.rem(middle + t, nh))
+        return at_place(1 - side, t - nh)
+
+    for t in range(gyn):
+        rows = pl.ds(pl.multiple_of(target(t) * zblk, zblk), zblk)
+        lanes = lax.broadcasted_iota(jnp.int32, (zblk, requests), 1).astype(F32)
+        chosen = jnp.where(row_of[rows, :1] == lanes, 1.0, 0.0).astype(BF16)
+        perm[t] = jnp.dot(
+            chosen, gath[...].reshape(requests, hl * HD), preferred_element_type=F32
+        ).astype(BF16)
+
+    def f_copy(n, t):
+        if t < nh:
+            return remote(
+                fsend.at[n, t - 1], frecv.at[n, t], fs.at[n, t], fr.at[n, t], gy=target(t)
+            )
+        return remote(fsend.at[n, t - 1], frecv.at[n, 0], fs.at[n, t], fr.at[n, 0], gy=target(t))
+
+    def m_copy(n, u, m):
+        return remote(
+            fsend.at[n, nh + u - 1], mrecv.at[n, u, m - 1], fs.at[n, nh + u], ms.at[n, u, m - 1],
+            gy=at_place(side, 0),
+        )
+
+    def merge(n):
+        @pl.when(middle == 0)
+        def _():
+            for u in range(nh):
+                total = fkeep[n, u]
+                for m in range(1, nh):
+                    m_copy(n, u, m).wait_recv()
+                    total = total + mrecv[n, u, m - 1].astype(F32)
+                fsend[n, nh + u - 1] = total.astype(BF16)
+                f_copy(n, nh + u).start()
 
     for n in range(NOUT):
         wo_copies[n].wait()
         rows = perm[...].reshape(requests, hl * HD)
         part = jnp.dot(rows, wobuf[n], preferred_element_type=F32)
-        for k in range(1, gyn):
-            fsend[n, k] = part[k * zblk : (k + 1) * zblk].astype(BF16)
-            f_copy(n, k).start()
         facc[n] = part[:zblk]
+        for u in range(nh):
+            fkeep[n, u] = part[(nh + u) * zblk : (nh + u + 1) * zblk]
+
+        @pl.when(middle > 0)
+        def _():
+            for u in range(nh):
+                fsend[n, nh + u - 1] = fkeep[n, u].astype(BF16)
+                m_copy(n, u, middle).start()
+
+        for t in range(1, nh):
+            fsend[n, t - 1] = part[t * zblk : (t + 1) * zblk].astype(BF16)
+            f_copy(n, t).start()
+        if n > 0:
+            merge(n - 1)
+    merge(NOUT - 1)
     for n in range(NOUT):
         total = facc[n]
-        for k in range(1, gyn):
-            f_copy(n, k).wait_recv()
-            total = total + frecv[n, k].astype(F32)
+        for t in range(nh):
+            f_copy(n, t if t > 0 else nh).wait_recv()
+            total = total + frecv[n, t].astype(F32)
         out[:, n * ow : (n + 1) * ow] = total.astype(BF16)
 
     sq_x.wait_send()
@@ -339,8 +414,8 @@
         for j in range(ny):
             c_copy(ypeer(j) * 2 + core, piece).wait_send()
     for n in range(NOUT):
-        for k in range(1, gyn):
-            f_copy(n, k).wait_send()
+        for t in range(1, gyn):
+            f_copy(n, t).wait_send()
 
 
 def body(gxn, gyn, hidden, cache_row, ctx_len, w_query, w_key, w_value, w_output, k_cache, v_cache):
@@ -356,20 +431,6 @@
     outw = w_output.shape[1]
     ow = outw // NOUT
 
-    first = (lax.axis_index("gx") * gyn + lax.axis_index("gy")) * rl
-    rows = first + jnp.arange(rl, dtype=jnp.int32)
-    lengths = jnp.sum(
-        jnp.where(cache_row[None, :] == rows[:, None], ctx_len[None, :], 0), axis=1
-    )
-    freq = jnp.exp(jnp.arange(HD // 2, dtype=F32) * (-2.0 * math.log(THETA) / HD))
-    angle = lengths.astype(F32)[:, None] * freq[None, :]
-    cosine = jnp.cos(angle)
-    sine = jnp.sin(angle)
-    cos2 = jnp.concatenate([cosine, cosine], axis=1)
-    sin2 = jnp.concatenate([-sine, sine], axis=1)
-    slot = jnp.arange(ctx + PAD, dtype=jnp.int32)[None, :]
-    bias = jnp.where((slot < lengths[:, None]) & (slot < ctx) | (slot == ctx), 0.0, -jnp.inf)
-
     vm = pl.BlockSpec(memory_space=pltpu.VMEM)
     hbm = pl.BlockSpec(memory_space=pl.ANY)
     dma = pltpu.SemaphoreType.DMA
@@ -377,7 +438,7 @@
     return pl.pallas_call(
         functools.partial(kernel, gxn, gyn),
         out_shape=jax.ShapeDtypeStruct((zblk, outw), BF16),
-        in_specs=[vm] * 6 + [hbm] * 6,
+        in_specs=[vm] * 3 + [hbm] * 6,
         out_specs=vm,
         scratch_shapes=[
             V((NCH, dl, cw), BF16),
@@ -390,22 +451,27 @@
             V((NCH, requests // 2, cw), BF16),
             V((NCH, requests // 2, cw), BF16),
             V((ny, blk, HD), F32),
-            V((NCH, ny, blk, cw), BF16),
-            V((NCH, ny, blk, cw), BF16),
-            V((NCH, blk, cw), F32),
+            V((NCH, ny - 1, blk, cw), BF16),
+            V((NCH, ny - 1, blk, cw), BF16),
             V((ny, blk, HD), F32),
             V((ny, blk, HD), F32),
             V((blk, 1), F32),
+            V((rl, HD), F32),
+            V((rl, HD), F32),
+            V((rl, ctx + PAD), F32),
             V((NCH, gyn, rl, cw), BF16),
             V((gyn, NCH, rl, cw), BF16),
             V((rl, hl, HD), F32),
             V((rl, hl, HD), F32),
             V((gyn, rl, hl * HD), BF16),
             V((gxn, gyn, rl, hl * HD), BF16),
+            V((requests, HD), F32),
             V((gyn, zblk, hl * HD), BF16),
-            V((NOUT, gyn, zblk, ow), BF16),
-            V((NOUT, gyn, zblk, ow), BF16),
+            V((NOUT, gyn - 1, zblk, ow), BF16),
+            V((NOUT, gyn // 2, zblk, ow), BF16),
+            V((NOUT, gyn // 2, gyn // 2 - 1, zblk, ow), BF16),
             V((NOUT, zblk, ow), F32),
+            V((NOUT, gyn // 2, zblk, ow), F32),
             dma((NCH + 1,)), dma((NOUT,)), dma((2,)),
             dma((NCH + 1,)), dma((NCH + 1,)),
             dma((NCH + 1, ny)), dma((NCH + 1, ny)),
@@ -413,7 +479,7 @@
             dma((gyn,)), dma((gyn,)),
             dma((ny, gyn)), dma((ny, gyn)),
             dma((ny, gyn)), dma((ny, gyn)),
-            dma((NOUT, gyn)), dma((NOUT, gyn)),
+            dma((NOUT, gyn)), dma((NOUT, gyn // 2)), dma((NOUT, gyn // 2, gyn // 2 - 1)),
         ],
         compiler_params=pltpu.CompilerParams(
             collective_id=0, has_side_effects=True, vmem_limit_bytes=60 * 1024 * 1024
@@ -422,7 +488,7 @@
             flops=2 * requests * dl * cols, bytes_accessed=2 * dl * cols, transcendentals=0
         ),
     )(
-        hidden, cache_row[None, :], cache_row.reshape(gyn, zblk, 1), cos2, sin2, bias,
+        hidden, cache_row[None, :], ctx_len[None, :],
         w_query, w_key, w_value, w_output, k_cache, v_cache,
     )
 

time: 69.6 us -> 62.2 us (0.89)
  Pallas kernels: 63.5 us -> 60.3 us
  other arithmetic: 2.37 us -> 0 us
  local copies, waits for them, and re-layouts: 3.21 us -> 1.67 us
    pallas_call x1, Pallas kernels: 63.5 us -> 60.3 us  [body(): pl.pallas_call(functools.partial(kernel, gxn, gyn), out_shape=jax.ShapeDt...]
    reshape x1 -> x0, local copies, waits for them, and re-layouts: 1.54 us -> none  [body(): cache_row.reshape(gyn, zblk, 1)]
    reduce_sum x1 -> x0, other arithmetic: 0.88 us -> none  [body(): jnp.sum(jnp.where(cache_row[None, :] == rows[:, None], ctx_len[None, :],...]
where the time goes in v2:
time: 62.2 us; the launch traced here: 62 us
  Pallas kernels  60.3 us (97%)
  local copies, waits for them, and re-layouts  1.67 us (3%)
    pallas_call x1, Pallas kernels, body(): pl.pallas_call(functools.partial(kernel, gxn, gyn), out_shape=jax.ShapeDt...  60.3 us
    unnamed x1, local copies, waits for them, and re-layouts  1.67 us

profile of v2, /device:TPU:0, one launch (start us, length us, event | category | flops | bytes accessed | tf_op | source)
XLA Modules:
  0.0 62.0 jit_solution(6479534533209680115)
XLA Ops:
  0.0 60.3 %shard_map.91 = bf16[64,2048]{1,0:T(8,128)(2,1)} custom-call(bf16[256,2048]{1,0:T(8,128)(2,1)} %hidden.1, s32[1,256]{1,0:T(1,128)} %bitcast.2, s32[1,256]{1,0:T(1,128)} %bitcast.3, bf16[2048,2048]{1,0:T(8,128)(2,1)} %w_query.1, bf16[2048,256]{1,0:T(8,128)(2,1)} %w_key.1, bf16[2048,256]{1,0:T(8,128)(2,1)} %w_value.1, bf16[2048,2048]{1,0:T(8,128)(2,1)} %w_output.1, ...), custom_call_target="tpu_custom_call" | custom-call | flops 2684354560 | bytes 10485760 | tf_op jit(solution)/shard_map/pallas_call | solution.py:438
  60.3 1.7 %copy.11 = bf16[64,2048]{1,0:T(8,128)(2,1)} copy(bf16[64,2048]{1,0:T(8,128)(2,1)} %shard_map.91) | data formatting | bytes 524288

commit v3 on v2

--- a/solution.py
+++ b/solution.py
@@ -19,7 +19,7 @@
 BF16 = jnp.bfloat16
 NCH = 5
 NOUT = 4
-AHEAD = 2
+AHEAD = 5
 PAD = 16
 
 

time: 62.2 us -> 63.6 us (1.023)
  Pallas kernels: 60.3 us -> 61.8 us
    pallas_call x1, Pallas kernels: 60.3 us -> 61.8 us  [body(): pl.pallas_call(functools.partial(kernel, gxn, gyn), out_shape=jax.ShapeDt...]
where the time goes in v3:
time: 63.6 us; the launch traced here: 63.5 us
  Pallas kernels  61.8 us (97%)
  local copies, waits for them, and re-layouts  1.67 us (3%)
    pallas_call x1, Pallas kernels, body(): pl.pallas_call(functools.partial(kernel, gxn, gyn), out_shape=jax.ShapeDt...  61.8 us
    unnamed x1, local copies, waits for them, and re-layouts  1.67 us

profile of v3, /device:TPU:0, one launch (start us, length us, event | category | flops | bytes accessed | tf_op | source)
XLA Modules:
  0.0 63.5 jit_solution(12660481385737675377)
XLA Ops:
  0.0 61.8 %shard_map.91 = bf16[64,2048]{1,0:T(8,128)(2,1)} custom-call(bf16[256,2048]{1,0:T(8,128)(2,1)} %hidden.1, s32[1,256]{1,0:T(1,128)} %bitcast.2, s32[1,256]{1,0:T(1,128)} %bitcast.3, bf16[2048,2048]{1,0:T(8,128)(2,1)} %w_query.1, bf16[2048,256]{1,0:T(8,128)(2,1)} %w_key.1, bf16[2048,256]{1,0:T(8,128)(2,1)} %w_value.1, bf16[2048,2048]{1,0:T(8,128)(2,1)} %w_output.1, ...), custom_call_target="tpu_custom_call" | custom-call | flops 2684354560 | bytes 10485760 | tf_op jit(solution)/shard_map/pallas_call | solution.py:438
  61.8 1.7 %copy.11 = bf16[64,2048]{1,0:T(8,128)(2,1)} copy(bf16[64,2048]{1,0:T(8,128)(2,1)} %shard_map.91) | data formatting | bytes 524288
